TPU v7x, 256 devices: a whole 4x4x8 slice. The times are simulated.
256 devices in a mesh: dp: 16 (over z, x_lo), tensor: 16 (over x_hi, y, core).
Axes of the slice: x: 4 (x_hi: 2, x_lo: 2; x = x_hi * 2 + x_lo), y: 4, z: 8, core: 2. Of those that a mesh axis runs over, the one named last changes fastest.
Arguments:
- inputs: bfloat16 [3072, 4096], P('dp'), may hold values from -6 to 6
- gate_pre: bfloat16 [3072, 14784], P('dp', 'tensor'), may hold values from -6 to 6
- up_pre: bfloat16 [3072, 14784], P('dp', 'tensor'), may hold values from -6 to 6
- grad_hidden: bfloat16 [3072, 14784], P('dp', 'tensor'), may hold values from -6 to 6
- gate_up_weight: bfloat16 [2, 4096, 14784], P(None, 'dp', 'tensor'), may hold values from -0.046875 to 0.046875
- moment_code: bfloat16 [2, 4096, 14784], P(None, 'dp', 'tensor'), may hold values from -1 to 1
- second_code: bfloat16 [2, 4096, 14784], P(None, 'dp', 'tensor'), may hold values from 0.049804688 to 1
- moment_scale: float32 [2, 16, 14784], P(None, 'dp', 'tensor'), may hold values from 0.0005 to 0.005
- second_scale: float32 [2, 16, 14784], P(None, 'dp', 'tensor'), may hold values from 2e-06 to 2e-05
Outputs:
- input_grad: bfloat16 [3072, 4096], P('dp', 'tensor')
- adam_step: float32 [2, 4096, 14784], P(None, 'dp', 'tensor')
- moment_code_new: bfloat16 [2, 4096, 14784], P(None, 'dp', 'tensor')
- second_code_new: bfloat16 [2, 4096, 14784], P(None, 'dp', 'tensor')
- moment_scale_new: float32 [2, 16, 14784], P(None, 'dp', 'tensor')
- second_scale_new: float32 [2, 16, 14784], P(None, 'dp', 'tensor')
All inputs are finite; a program needn't handle non-finite values. Where the computation divides by a largest or mean magnitude, that divisor is 1e-20 or more.
Results may differ from a plain program's by a relative error of at most 0.025.
Values may be sent and summed in bfloat16 or wider, within the bound.
A program may use at most 128 MiB of HBM per device.

v0:
```python
import jax
import jax.numpy as jnp
from jax import lax
from jax.sharding import PartitionSpec as P

BLOCK = 256


beta_first = 0.9
beta_second = 0.95
bias_first = 0.19
bias_second = 0.0975
adam_eps = 1e-08
scale_eps = 1e-06


def dequantize(block_code, block_scale):
    row_count, width = block_code.shape
    blocks = block_code.astype(jnp.float32).reshape(-1, BLOCK, width)
    return (blocks * block_scale[:, None, :]).reshape(row_count, width)


def requantize(values):
    row_count, width = values.shape
    blocks = values.reshape(-1, BLOCK, width)
    block_scale = jnp.max(jnp.abs(blocks), axis=1) + scale_eps
    block_code = (blocks / block_scale[:, None, :]).reshape(row_count, width).astype(jnp.bfloat16)
    return (block_code, block_scale)


def adam_update(weight_grad, moment_code, second_code, moment_scale, second_scale):
    moment = beta_first * dequantize(moment_code, moment_scale) + (1.0 - beta_first) * weight_grad
    second = (
        beta_second * dequantize(second_code, second_scale)
        + (1.0 - beta_second) * weight_grad * weight_grad
    )
    adam_step = moment / bias_first / (jnp.sqrt(second / bias_second) + adam_eps)
    moment_code_new, moment_scale_new = requantize(moment)
    second_code_new, second_scale_new = requantize(second)
    return (adam_step, moment_code_new, second_code_new, moment_scale_new, second_scale_new)


def per_device(
    inputs,
    gate_pre,
    up_pre,
    grad_hidden,
    gate_up_weight,
    moment_code,
    second_code,
    moment_scale,
    second_scale,
):
    gate = gate_pre.astype(jnp.float32)
    upper = up_pre.astype(jnp.float32)
    incoming = grad_hidden.astype(jnp.float32)
    sigmoid_gate = jax.nn.sigmoid(gate)
    grad_up = (incoming * gate * sigmoid_gate).astype(jnp.bfloat16)
    grad_gate = (incoming * upper * sigmoid_gate * (1.0 + gate * (1.0 - sigmoid_gate))).astype(
        jnp.bfloat16
    )
    paired = jnp.concatenate([grad_gate, grad_up], axis=1)
    stacked = jnp.stack([grad_gate, grad_up])
    tok_rows = inputs.shape[0]
    owned_rows = gate_up_weight.shape[1]
    hidden_local = gate_up_weight.shape[2]
    token_total = tok_rows * lax.axis_size("dp")
    partial_sums = jnp.einsum(
        "ptf,prf->tr",
        stacked,
        lax.all_gather(gate_up_weight, "dp", axis=1, tiled=True),
        preferred_element_type=jnp.float32,
    )
    input_grad = lax.psum_scatter(partial_sums, "tensor", scatter_dimension=1, tiled=True).astype(
        jnp.bfloat16
    )
    owned_columns = lax.all_to_all(inputs, "dp", split_axis=1, concat_axis=0, tiled=True)
    shard_piece = lax.all_gather(paired, "dp", axis=0, tiled=True)
    row_count = shard_piece.shape[0]
    block_count = row_count // tok_rows
    terms = jnp.einsum(
        "ktr,ktf->krf",
        owned_columns.reshape(block_count, tok_rows, owned_rows),
        shard_piece.reshape(block_count, tok_rows, 2 * hidden_local),
        preferred_element_type=jnp.float32,
    )
    rounded = lax.optimization_barrier(terms.astype(jnp.bfloat16)).astype(jnp.float32)
    summed = jnp.sum(rounded, axis=0)
    summed = summed / token_total
    weight_grad = jnp.stack([summed[:, :hidden_local], summed[:, hidden_local:]])
    results = jax.vmap(adam_update)(
        weight_grad, moment_code, second_code, moment_scale, second_scale
    )
    return (input_grad, results[0], results[1], results[2], results[3], results[4])


def solution(mesh):
    return jax.shard_map(
        per_device,
        mesh=mesh,
        in_specs=(
            P("dp", None),
            P("dp", "tensor"),
            P("dp", "tensor"),
            P("dp", "tensor"),
            P(None, "dp", "tensor"),
            P(None, "dp", "tensor"),
            P(None, "dp", "tensor"),
            P(None, "dp", "tensor"),
            P(None, "dp", "tensor"),
        ),
        out_specs=(
            P("dp", "tensor"),
            P(None, "dp", "tensor"),
            P(None, "dp", "tensor"),
            P(None, "dp", "tensor"),
            P(None, "dp", "tensor"),
            P(None, "dp", "tensor"),
        ),
        check_vma=False,
    )
```

profile of v0, /device:TPU:6, one launch (start us, length us, event | category | flops | bytes accessed | tf_op | source)
XLA Modules:
  0.0 730.8 jit_solution(16256055494454690252)
XLA Ops:
  7.2 0.0 copy-start.3
  7.2 0.0 copy-start.4
  7.2 0.0 copy-start.5
  7.2 0.0 all-gather.3.cloned.1.call-start
  7.2 2.3 copy.21
  9.6 0.0 all-gather.3.cloned.1.call-update
  9.6 0.0 copy-start.2
  9.6 0.0 all-gather.5.cloned.1.call-start
  9.7 0.0 copy-done.3
  9.7 0.0 copy-done.4
  9.7 0.0 copy-done.5
  9.7 0.4 fusion.4
  10.1 1.1 pad_maximum_fusion.1
  11.2 0.0 all-gather.5.cloned.1.call-update
  11.2 0.0 copy-done.2
  11.2 1.3 copy.48
  12.5 0.0 copy-start.6
  12.5 0.0 copy-start.7
  12.5 10.1 %all-to-all-start = ((bf16[192,16,256]{2,0,1:T(8,128)(2,1)}), bf16[192,16,256]{2,0,1:T(8,128)(2,1)S(1)}, u32[]{:S(2)}, u32[]{:S(2)}) async-start(bf16[192,16,256]{2,0,1:T(8,128)(2,1)} %bitcast.23), calls=%async_computation.1 | async-start | bytes 3145728 | tf_op jit(solution)/shard_map/all_to_all | solution.py:77
  22.6 0.0 reduce-scatter.2.cloned.1.call-start
  22.7 0.0 copy-done.6
  22.7 0.0 copy-done.7
  22.7 354.6 %all-gather.3.cloned.1.call-done = bf16[2,4096,924]{1,2,0:T(8,128)(2,1)} async-done(((bf16[2,256,924]{1,2,0:T(8,128)(2,1)}), bf16[2,4096,924]{1,2,0:T(8,128)(2,1)}) %all-gather.3.cloned.1.call-update) | async-done | bytes 15138832 | tf_op jit(solution)/shard_map/all_gather | solution.py:71
  377.3 10.5 %convolution_bitcast_fusion = f32[192,4096]{1,0:T(8,128)} fusion(bf16[2,4096,924]{1,2,0:T(8,128)(2,1)} %all-gather.3.cloned.1.call-done, bf16[1,192,924]{2,1,0:T(8,128)(2,1)S(1)} %bitcast.29, bf16[1,192,924]{2,1,0:T(8,128)(2,1)S(1)} %bitcast.28), kind=kOutput, calls=%fused_computation.2 | convolution fusion | flops 2907007488 | bytes 18994176 | tf_op jit(solution)/shard_map/ptf,prf->tr/dot_general | solution.py:68
  387.7 0.0 reduce-scatter.2.cloned.1.call-update
  387.7 0.0 all-to-all-done
  387.8 247.1 %all-gather.5.cloned.1.call-done = bf16[3072,1848]{1,0:T(8,128)(2,1)} async-done(((bf16[192,1848]{1,0:T(8,128)(2,1)}), bf16[3072,1848]{1,0:T(8,128)(2,1)}) %all-gather.5.cloned.1.call-update) | async-done | bytes 11354128 | tf_op jit(solution)/shard_map/all_gather | solution.py:78
  634.8 10.9 %convert_bitcast_fusion = bf16[16,256,1848]{1,2,0:T(8,128)(2,1)} fusion(bf16[16,192,1848]{2,1,0:T(8,128)(2,1)} %bitcast.26, bf16[192,16,256]{2,0,1:T(8,128)(2,1)S(1)} %all-to-all-done), kind=kOutput, calls=%fused_computation.1 | convolution fusion | flops 2914222080 | bytes 28065792 | tf_op jit(solution)/shard_map/ktr,ktf->krf/dot_general | solution.py:81
  645.7 6.4 convert_reduce_fusion
  652.1 0.2 broadcast_multiply_fusion
  652.2 0.0 copy-start
  652.3 0.0 copy-start.1
  652.3 0.1 slice_bitcast_fusion.1
  652.4 1.1 copy-done
  653.5 0.3 copy-done.1
  653.8 2.4 abs_reduce_fusion
  656.2 2.7 copy.25
  658.9 0.6 add.72
  659.5 0.6 add.73
  660.1 1.4 divide_convert_fusion
  661.5 1.9 copy.26
  663.4 1.9 copy.27
  665.3 57.4 %reduce-scatter.2.cloned.1.call-done = f32[192,256]{1,0:T(8,128)} async-done(((f32[192,4096]{1,0:T(8,128)}), f32[192,256]{1,0:T(8,128)}) %reduce-scatter.2.cloned.1.call-update) | async-done | bytes 196624 | tf_op jit(solution)/shard_map/reduce_scatter | solution.py:74
  722.7 1.6 convert_element_type.44
  (3 shorter events, 0.0 us)
Async XLA Ops:
  7.2 2.5 copy-start.3
  7.2 2.5 copy-start.4
  7.2 2.5 copy-start.5
  7.2 370.1 %all-gather.3.cloned.1.call-start = ((), (), s32[]{:S(2)}) async-start(), calls=%async_computation.2 | async-start | bytes 16154624 | tf_op jit(solution)/shard_map/all_gather | solution.py:71
  9.6 1.6 copy-start.2
  9.6 625.2 %all-gather.5.cloned.1.call-start = ((), (), s32[]{:S(2)}) async-start(), calls=%async_computation.4 | async-start | bytes 12533760 | tf_op jit(solution)/shard_map/all_gather | solution.py:78
  12.5 10.1 %copy-start.6 = (f32[2,1,924]{2,1,0:T(1,128)S(1)}, f32[2,1,924]{2,1,0:T(1,128)}, u32[]{:S(2)}) copy-start(f32[2,1,924]{2,1,0:T(1,128)} %param.17) | copy-start | bytes 22180
  12.5 10.1 %copy-start.7 = (f32[2,1,924]{2,1,0:T(1,128)S(1)}, f32[2,1,924]{2,1,0:T(1,128)}, u32[]{:S(2)}) copy-start(f32[2,1,924]{2,1,0:T(1,128)} %param.16) | copy-start | bytes 22180
  12.5 375.2 %all-to-all-start = ((bf16[192,16,256]{2,0,1:T(8,128)(2,1)}), bf16[192,16,256]{2,0,1:T(8,128)(2,1)S(1)}, u32[]{:S(2)}, u32[]{:S(2)}) async-start(bf16[192,16,256]{2,0,1:T(8,128)(2,1)} %bitcast.23), calls=%async_computation.1 | async-start | bytes 3145728 | tf_op jit(solution)/shard_map/all_to_all | solution.py:77
  22.6 700.1 %reduce-scatter.2.cloned.1.call-start = ((), (), s32[]{:S(2)}) async-start(), calls=%async_computation.3 | async-start | bytes 3342336 | tf_op jit(solution)/shard_map/reduce_scatter | solution.py:74
  652.2 1.2 copy-start
  652.3 1.6 copy-start.1
Sparse Core Ops, SparseCore 0:
  9.7 367.4 all-gather.2
  379.6 255.1 all-gather.4
  639.2 83.4 reduce-scatter.1
where the time goes:
time: 732 us; the launch traced here: 731 us
  waiting for transfers between devices  659 us (90%)
  matrix products  21.3 us (3%)
  between operations  13.9 us (2%)
  other arithmetic  13.4 us (2%)
  local copies, waits for them, and re-layouts  13 us (2%)
  starting transfers between devices  10.2 us (1%)
    all_gather x1, waiting for transfers between devices, per_device(): lax.all_gather(gate_up_weight, 'dp', axis=1, tiled=True)  355 us
    all_gather x1, waiting for transfers between devices, per_device(): shard_piece = lax.all_gather(paired, 'dp', axis=0, tiled=True)  247 us
    reduce_scatter x1, waiting for transfers between devices, per_device(): lax.psum_scatter(partial_sums, 'tensor', scatter_dimension=1, tiled=True)  57.4 us
  transfers between devices with their start and end apart: 4, of which 3 were waited for; matrix products, arithmetic and copies ran while one was open for 6% of the time, Pallas kernels for 0%

commit v1 on v0

v1 whole, which is shorter than its diff:
```python
import functools

import jax
import jax.numpy as jnp
from jax import lax
from jax.experimental import pallas as pl
from jax.experimental.pallas import tpu as pltpu
from jax.sharding import PartitionSpec as P

MESH = pl.DeviceIdType.MESH
F32 = jnp.float32
BF16 = jnp.bfloat16

beta_first = 0.9
beta_second = 0.95
bias_first = 0.19
bias_second = 0.0975
adam_eps = 1e-08
scale_eps = 1e-06

TOK = 192
HALF = 96
ROWS = 256
HID = 924
PACK = 1920
NZ = 8
NM = 8
TOKENS = 3072
QR = 48
LANE = 128

GROUPS = ((0, 384, 0), (384, 384, 768), (768, 128, 1536))
TAIL_AT = 1792
TAIL_FROM = 896
TAIL = HID - TAIL_FROM
CHUNKS = ((0, 768), (768, 768), (1536, 384))
LAST = len(CHUNKS) - 1


def slot_of(rel):
    rel = rel % NZ
    if rel == 0:
        return 0
    if rel == 4:
        return 7
    return 2 * rel if rel < 4 else 2 * (NZ - rel) - 1


REL_OF = {slot_of(rel): rel for rel in range(NZ)}
ROUNDS = ((0, 3), (3, 5), (5, 7), (7, 8))


def pack_tail(first, second):
    rows = first.shape[0]
    blank = jnp.zeros((rows, 64 - TAIL), first.dtype)
    return jnp.concatenate([first, blank, second, blank], axis=1)


def comm_kernel(
    x_hbm, gate_hbm, up_hbm, gh_hbm, w_hbm,
    wg_hbm, out_hbm,
    gate_v, up_v, gh_v, w_v, gbuf, xbuf, xt, wbuf, wt,
    dw_send, dw_recv, dw_own, c_send, c_recv, keep, rs_src, rs_recv, f_src, f_buf,
    load_sem, ring_s, ring_r, x1_s, x1_r, x2_s, x2_r, x3_s, x3_r, w_s, w_r,
    dw_s, dw_r, core_s, core_r, rs_s, rs_r, fin_s, fin_r, out_sem,
):
    d = lax.axis_index("dp")
    t = lax.axis_index("tensor")
    z, xl = d // 2, d % 2
    m, c = t // 2, t % 2
    y, xh = m % 4, m // 4

    def at_z(r):
        return (((z + r) % NZ) * 2 + xl, t)

    def at_m(e):
        return (d, ((m + e) % NM) * 2 + c)

    sibling = (d, m * 2 + (1 - c))
    partner = (z * 2 + (1 - xl), t)

    loads = [
        pltpu.make_async_copy(gate_hbm, gate_v, load_sem.at[0]),
        pltpu.make_async_copy(up_hbm, up_v, load_sem.at[1]),
        pltpu.make_async_copy(gh_hbm, gh_v, load_sem.at[2]),
        pltpu.make_async_copy(w_hbm, w_v, load_sem.at[3]),
    ]
    for load in loads:
        load.start()

    barrier = pltpu.get_barrier_semaphore()
    for r in range(1, NZ):
        pl.semaphore_signal(barrier, inc=1, device_id=at_z(r), device_id_type=MESH)
    for e in range(1, NM):
        pl.semaphore_signal(barrier, inc=1, device_id=at_m(e), device_id_type=MESH)
    pl.semaphore_signal(barrier, inc=1, device_id=sibling, device_id_type=MESH)
    pl.semaphore_signal(barrier, inc=1, device_id=partner, device_id_type=MESH)
    for source in range(NM):
        pl.semaphore_signal(
            barrier, inc=1, device_id=(m * 2 + xl, source * 2 + c), device_id_type=MESH
        )
    pl.semaphore_wait(barrier, 2 * (NZ - 1) + 2 + NM)

    sends = []

    def remote(src, dst, send_sem, recv_sem, where):
        return pltpu.make_async_remote_copy(
            src_ref=src, dst_ref=dst, send_sem=send_sem, recv_sem=recv_sem,
            device_id=where, device_id_type=MESH,
        )

    def launch(copy):
        copy.start()
        sends.append(copy)
        return copy

    q_at = pl.multiple_of(y * QR, 16)
    ct_at = pl.multiple_of((c * 2 + xh) * LANE, LANE)

    def x_columns(r):
        return pl.ds(pl.multiple_of(((z + r) % NZ) * 512 + (c * 2 + xh) * LANE, LANE), LANE)

    x_first = []
    for r in range(1, NZ):
        x_first.append(launch(remote(
            x_hbm.at[pl.ds(q_at, QR), x_columns(r)],
            xbuf.at[slot_of(-r), pl.ds(q_at, QR), pl.ds(ct_at, LANE)],
            x1_s.at[r], x1_r.at[r], at_z(r),
        )))
    x_own = pltpu.make_async_copy(
        x_hbm.at[pl.ds(q_at, QR), x_columns(0)],
        xbuf.at[0, pl.ds(q_at, QR), pl.ds(ct_at, LANE)], x1_r.at[0],
    )
    x_own.start()

    ring = {}
    for k, (start, width) in enumerate(CHUNKS):
        for s in range(1, 5):
            for way in range(2):
                for h in range(2):
                    if s == 4 and way != h:
                        continue
                    sign = -1 if way == 0 else 1
                    src_slot, dst_slot = slot_of(sign * (s - 1)), slot_of(sign * s)
                    rows, columns = pl.ds(h * HALF, HALF), pl.ds(start, width)
                    ring[k, s, way, h] = remote(
                        gbuf.at[src_slot, rows, columns],
                        gbuf.at[dst_slot, rows, columns],
                        ring_s.at[k, s - 1, way, h], ring_r.at[k, s - 1, way, h],
                        at_z(1 if way == 0 else -1),
                    )

    def grads(first, width):
        g = gate_v[:, first:first + width].astype(F32)
        u = up_v[:, first:first + width].astype(F32)
        h = gh_v[:, first:first + width].astype(F32)
        sig = jax.nn.sigmoid(g)
        g_up = (h * g * sig).astype(BF16)
        g_gate = (h * u * sig * (1.0 + g * (1.0 - sig))).astype(BF16)
        return g_gate, g_up

    def fill(k):
        first, width, at = GROUPS[k]
        g_gate, g_up = grads(first, width)
        gbuf[0, :, at:at + width] = g_gate
        gbuf[0, :, at + width:at + 2 * width] = g_up
        if k == LAST:
            g_gate, g_up = grads(TAIL_FROM, TAIL)
            gbuf[0, :, TAIL_AT:TAIL_AT + LANE] = pack_tail(g_gate, g_up)

    def first_step(k):
        for h in range(2):
            for way in range(2):
                launch(ring[k, 1, way, h])

    for load in loads[:3]:
        load.wait()
    fill(0)
    first_step(0)

    loads[3].wait()
    for first, width, at in GROUPS:
        wbuf[0, :, at:at + width] = w_v[0, :, first:first + width]
        wbuf[0, :, at + width:at + 2 * width] = w_v[1, :, first:first + width]
    wbuf[0, :, TAIL_AT:TAIL_AT + LANE] = pack_tail(
        w_v[0, :, TAIL_FROM:HID], w_v[1, :, TAIL_FROM:HID]
    )
    w_copy = launch(remote(wbuf.at[0], wbuf.at[1], w_s, w_r, partner))

    fill(1)

    def x_second():
        x_own.wait()
        for copy in x_first:
            copy.wait_recv()
        piece = xbuf.at[:, pl.ds(q_at, QR), pl.ds(ct_at, LANE)]
        for e in range(1, NM):
            launch(remote(piece, piece, x2_s.at[e], x2_r.at[e], at_m(e)))

    def x_third():
        for e in range(1, NM):
            src_m = (m + NM - e) % NM
            there = xbuf.at[
                :,
                pl.ds(pl.multiple_of((src_m % 4) * QR, 16), QR),
                pl.ds(pl.multiple_of((c * 2 + src_m // 4) * LANE, LANE), LANE),
            ]
            remote(there, there, x2_s.at[e], x2_r.at[e], at_m(e)).wait_recv()
        mine = xbuf.at[:, :, pl.ds(pl.multiple_of(c * 256, 256), 256)]
        launch(remote(mine, mine, x3_s, x3_r, sibling))

    def x_turn():
        theirs = xbuf.at[:, :, pl.ds(pl.multiple_of((1 - c) * 256, 256), 256)]
        remote(theirs, theirs, x3_s, x3_r, sibling).wait_recv()
        for j in range(2):
            for i in range(4):
                block = xbuf[2 * i:2 * i + 2, :, j * 256:(j + 1) * 256].reshape(2 * TOK, 256)
                xt[j, :, i * 2 * TOK:(i + 1) * 2 * TOK] = block.T

    def w_turn():
        w_copy.wait_recv()
        for which in range(2):
            j = xl if which == 0 else 1 - xl
            for i in range(5):
                wt[j, i * 384:(i + 1) * 384, :] = wbuf[which, :, i * 384:(i + 1) * 384].T

    dw_copies = {}

    def dw_product(j, first, width):
        block = gbuf[:, :, first:first + width].reshape(NZ * TOK, width)
        return jnp.dot(xt[j], block, preferred_element_type=F32)

    def dw_out(k):
        start, width = CHUNKS[k]
        for first in range(start, start + width, 384):
            dw_send[:, first:first + 384] = dw_product(1 - xl, first, 384).astype(BF16)
        columns = pl.ds(start, width)
        dw_copies[k] = launch(remote(
            dw_send.at[:, columns], dw_recv.at[:, columns], dw_s.at[k], dw_r.at[k], partner
        ))

    def dw_keep(k):
        start, width = CHUNKS[k]
        for first in range(start, start + width, 384):
            dw_own[:, first:first + 384] = dw_product(xl, first, 384)

    wg_copies = []

    def dw_end(k):
        start, width = CHUNKS[k]
        dw_copies[k].wait_recv()
        for first in range(start, start + width, 384):
            columns = slice(first, first + 384)
            dw_own[:, columns] = (dw_own[:, columns] + dw_recv[:, columns].astype(F32)) / TOKENS
        columns = pl.ds(start, width)
        copy = pltpu.make_async_copy(dw_own.at[:, columns], wg_hbm.at[:, columns], out_sem.at[k])
        copy.start()
        wg_copies.append(copy)

    core_copies = {}
    rs_copies = {}

    def dx_product(n):
        lo, hi = ROUNDS[n]
        block = gbuf[lo:hi].reshape((hi - lo) * TOK, PACK)
        there = jnp.dot(block, wt[1 - c], preferred_element_type=F32).astype(BF16)
        c_send[lo:hi] = there.reshape(hi - lo, TOK, 256)
        core_copies[n] = launch(remote(
            c_send.at[lo:hi], c_recv.at[lo:hi], core_s.at[n], core_r.at[n], sibling
        ))
        keep[lo:hi] = jnp.dot(block, wt[c], preferred_element_type=F32).reshape(hi - lo, TOK, 256)

    def dx_scatter(n):
        lo, hi = ROUNDS[n]
        core_copies[n].wait_recv()
        rs_src[lo:hi] = (keep[lo:hi] + c_recv[lo:hi].astype(F32)).astype(BF16)
        for e in range(1, NM):
            to = (m + e) % NM
            rs_copies[n, e] = launch(remote(
                rs_src.at[
                    lo:hi,
                    pl.ds(pl.multiple_of((to % 4) * QR, 16), QR),
                    pl.ds(pl.multiple_of((to // 4) * LANE, LANE), LANE),
                ],
                rs_recv.at[e, lo:hi],
                rs_s.at[n, e], rs_r.at[n, e], at_m(e),
            ))

    x_at = pl.multiple_of(xh * LANE, LANE)
    home = z == m
    fin_copies = {}

    def dx_finish(n):
        lo, hi = ROUNDS[n]
        for e in range(1, NM):
            rs_copies[n, e].wait_recv()
        total = rs_src[lo:hi, pl.ds(q_at, QR), pl.ds(x_at, LANE)].astype(F32)
        for e in range(1, NM):
            total = total + rs_recv[e, lo:hi].astype(F32)
        f_src[lo:hi] = total.astype(BF16)
        for p in range(lo, hi):
            rel = REL_OF[p]
            there = f_buf.at[pl.ds(q_at, QR), pl.ds(x_at, LANE)]
            copy = remote(
                f_src.at[p], there, fin_s.at[p], fin_r,
                (((z + rel) % NZ) * 2 + xl, z * 2 + c),
            )
            if rel:
                launch(copy)
            else:
                local = pltpu.make_async_copy(f_src.at[p], there, fin_r)
                pl.when(home)(local.start)
                pl.when(jnp.logical_not(home))(copy.start)
                fin_copies[0] = copy

    def after(k, s):
        if k == 0:
            if s == 1:
                x_second()
                fill(LAST)
            elif s == 2:
                x_third()
            elif s == 3:
                x_turn()
        elif k == 1:
            if s == 1:
                dw_out(0)
            elif s == 2:
                dw_keep(0)
            elif s == 3:
                w_turn()
            else:
                dw_end(0)
        else:
            if s == 1:
                dw_out(1)
                dx_product(0)
            elif s == 2:
                dx_scatter(0)
                dw_keep(1)
                dx_product(1)
            elif s == 3:
                dx_scatter(1)
                dx_finish(0)
                dx_product(2)
            else:
                dx_product(3)
                dw_out(2)
                dx_scatter(2)
                dx_scatter(3)
                dw_keep(2)
                dw_end(1)
                dx_finish(1)
                dx_finish(2)
                dx_finish(3)
                dw_end(2)

    for k in range(len(CHUNKS)):
        for s in range(1, 5):
            for h in range(2):
                for way in range(2):
                    if (k, s, way, h) not in ring:
                        continue
                    ring[k, s, way, h].wait_recv()
                    if (k, s + 1, way, h) in ring:
                        launch(ring[k, s + 1, way, h])
            if s == 3 and k < LAST:
                first_step(k + 1)
            after(k, s)

    pltpu.make_async_copy(f_buf, f_buf, fin_r).wait()
    result = pltpu.make_async_copy(f_buf, out_hbm, out_sem.at[LAST + 1])
    result.start()
    for copy in sends:
        copy.wait_send()
    pl.when(jnp.logical_not(home))(fin_copies[0].wait_send)
    for copy in wg_copies:
        copy.wait()
    result.wait()


def communicate(x, gate, up, gh, w):
    any_spec = pl.BlockSpec(memory_space=pl.ANY)
    dma = pltpu.SemaphoreType.DMA
    n = len(CHUNKS)
    return pl.pallas_call(
        comm_kernel,
        out_shape=(
            jax.ShapeDtypeStruct((ROWS, PACK), F32),
            jax.ShapeDtypeStruct((TOK, 256), BF16),
        ),
        in_specs=[any_spec] * 5,
        out_specs=(any_spec, any_spec),
        scratch_shapes=[
            pltpu.VMEM((TOK, HID), BF16),
            pltpu.VMEM((TOK, HID), BF16),
            pltpu.VMEM((TOK, HID), BF16),
            pltpu.VMEM((2, ROWS, HID), BF16),
            pltpu.VMEM((NZ, TOK, PACK), BF16),
            pltpu.VMEM((NZ, TOK, 512), BF16),
            pltpu.VMEM((2, 256, NZ * TOK), BF16),
            pltpu.VMEM((2, ROWS, PACK), BF16),
            pltpu.VMEM((2, PACK, 256), BF16),
            pltpu.VMEM((ROWS, PACK), BF16),
            pltpu.VMEM((ROWS, PACK), BF16),
            pltpu.VMEM((ROWS, PACK), F32),
            pltpu.VMEM((NZ, TOK, 256), BF16),
            pltpu.VMEM((NZ, TOK, 256), BF16),
            pltpu.VMEM((NZ, TOK, 256), F32),
            pltpu.VMEM((NZ, TOK, 256), BF16),
            pltpu.VMEM((NM, NZ, QR, LANE), BF16),
            pltpu.VMEM((NZ, QR, LANE), BF16),
            pltpu.VMEM((TOK, 256), BF16),
            dma((4,)),
            dma((n, 4, 2, 2)), dma((n, 4, 2, 2)),
            dma((NZ,)), dma((NZ,)),
            dma((NM,)), dma((NM,)),
            dma, dma, dma, dma,
            dma((n,)), dma((n,)),
            dma((4,)), dma((4,)),
            dma((4, NM)), dma((4, NM)),
            dma((NZ,)), dma,
            dma((n + 1,)),
        ],
        compiler_params=pltpu.CompilerParams(
            collective_id=0, has_side_effects=True, vmem_limit_bytes=48 * 1024 * 1024
        ),
        cost_estimate=pl.CostEstimate(
            flops=6_000_000_000, bytes_accessed=8_000_000, transcendentals=200_000
        ),
    )(x, gate, up, gh, w)


def adam_kernel(wg, mc, sc, ms, ss, step, mc_new, sc_new, ms_new, ss_new):
    p = pl.program_id(0)

    def piece(first, width, grad):
        columns = slice(first, first + width)
        moment = beta_first * (mc[0, :, columns].astype(F32) * ms[0, :, columns])
        moment = moment + (1.0 - beta_first) * grad
        second = beta_second * (sc[0, :, columns].astype(F32) * ss[0, :, columns])
        second = second + (1.0 - beta_second) * grad * grad
        step[0, :, columns] = moment / bias_first / (jnp.sqrt(second / bias_second) + adam_eps)
        m_scale = jnp.max(jnp.abs(moment), axis=0, keepdims=True) + scale_eps
        s_scale = jnp.max(jnp.abs(second), axis=0, keepdims=True) + scale_eps
        ms_new[0, :, columns] = m_scale
        ss_new[0, :, columns] = s_scale
        mc_new[0, :, columns] = (moment / m_scale).astype(BF16)
        sc_new[0, :, columns] = (second / s_scale).astype(BF16)

    for first, width, at in GROUPS:
        for inner in range(0, width, LANE):
            begin = pl.multiple_of(at + inner + p * width, LANE)
            piece(first + inner, LANE, wg[:, pl.ds(begin, LANE)])
    tail = wg[:, TAIL_AT:TAIL_AT + LANE]
    tail = jnp.where(p == 0, tail, pltpu.roll(tail, 64, 1))
    piece(TAIL_FROM, TAIL, tail[:, :TAIL])


def adam(wg, mc, sc, ms, ss):
    big = pl.BlockSpec((1, ROWS, HID), lambda p: (p, 0, 0))
    small = pl.BlockSpec((1, 1, HID), lambda p: (p, 0, 0))
    return pl.pallas_call(
        adam_kernel,
        grid=(2,),
        out_shape=(
            jax.ShapeDtypeStruct((2, ROWS, HID), F32),
            jax.ShapeDtypeStruct((2, ROWS, HID), BF16),
            jax.ShapeDtypeStruct((2, ROWS, HID), BF16),
            jax.ShapeDtypeStruct((2, 1, HID), F32),
            jax.ShapeDtypeStruct((2, 1, HID), F32),
        ),
        in_specs=[pl.BlockSpec((ROWS, PACK), lambda p: (0, 0)), big, big, small, small],
        out_specs=(big, big, big, small, small),
        compiler_params=pltpu.CompilerParams(vmem_limit_bytes=32 * 1024 * 1024),
    )(wg, mc, sc, ms, ss)


def per_device(x, gate, up, gh, w, mc, sc, ms, ss):
    wg, input_grad = communicate(x, gate, up, gh, w)
    return (input_grad,) + tuple(adam(wg, mc, sc, ms, ss))


def solution(mesh):
    whole = P(None, "dp", "tensor")
    token = P("dp", "tensor")
    return jax.shard_map(
        per_device,
        mesh=mesh,
        in_specs=(P("dp", None), token, token, token, whole, whole, whole, whole, whole),
        out_specs=(token, whole, whole, whole, whole, whole),
        check_vma=False,
    )
```

time: 732 us -> 138 us (0.19)
  waiting for transfers between devices: 659 us -> 0 us
  Pallas kernels: 0 us -> 114 us
  matrix products: 21.3 us -> 0 us
  other arithmetic: 13.4 us -> 0 us
  between operations: 13.9 us -> 0.75 us
  starting transfers between devices: 10.2 us -> 0 us
  local copies, waits for them, and re-layouts: 13 us -> 22.9 us
    all_gather x2 -> x0, waiting for transfers between devices: 602 us -> none  [the longest x1 355 us: per_device(): lax.all_gather(gate_up_weight, 'dp', axis=1, tiled=True)]
    pallas_call x0 -> x2, Pallas kernels: none -> 114 us  [the longest x1 111 us: communicate(): pl.pallas_call(comm_kernel, out_shape=(jax.ShapeDtypeStruct((ROWS, PACK),...]
    reduce_scatter x1 -> x0, waiting for transfers between devices: 57.4 us -> none  [per_device(): lax.psum_scatter(partial_sums, 'tensor', scatter_dimension=1, tiled=True)]
    dot_general x2 -> x0, matrix products: 21.3 us -> none  [the longest x1 10.9 us: per_device(): jnp.einsum('ktr,ktf->krf', owned_columns.reshape(block_count, tok_rows, o...]
    unnamed x22 -> x31, local copies, waits for them, and re-layouts: 10.3 us -> 22.9 us
    all_to_all x1 -> x0, starting transfers between devices: 10.1 us -> none  [per_device(): lax.all_to_all(inputs, 'dp', split_axis=1, concat_axis=0, tiled=True)]
  transfers between devices with their start and end apart: 4 -> 0, of which waited for: 3 -> 0; matrix products, arithmetic and copies ran while one was open for 6% -> 0% of each run, Pallas kernels for 0% -> 0%
where the time goes in v1:
time: 138 us; the launch traced here: 137 us
  Pallas kernels  114 us (83%)
  local copies, waits for them, and re-layouts  22.9 us (17%)
    pallas_call x1, Pallas kernels, communicate(): pl.pallas_call(comm_kernel, out_shape=(jax.ShapeDtypeStruct((ROWS, PACK),...  111 us
    unnamed x31, local copies, waits for them, and re-layouts  22.9 us
    pallas_call x1, Pallas kernels, adam(): pl.pallas_call(adam_kernel, grid=(2,), out_shape=(jax.ShapeDtypeStruct((2...  3.08 us

profile of v1, /device:TPU:6, one launch (start us, length us, event | category | flops | bytes accessed | tf_op | source)
XLA Modules:
  0.0 137.4 jit_solution(11679742520591992248)
XLA Ops:
  0.6 0.0 copy-start.8
  0.6 0.0 copy-start.7
  0.7 2.6 %copy.15.w_hbm = bf16[2,256,924]{2,1,0:T(8,128)(2,1)S(1)} copy(bf16[2,256,924]{1,0,2:T(2,128)(2,1)} %param.13) | data formatting | bytes 1892352 | tf_op args[4]
  3.2 0.0 copy-done.8
  3.3 0.0 copy-done.7
  3.3 0.0 copy-start.9
  3.3 1.0 copy-done.9
  4.3 0.0 copy-start.10
  4.3 1.0 copy-done.10
  5.3 110.7 %shard_map.136 = (f32[256,1920]{1,0:T(8,128)S(1)}, bf16[192,256]{1,0:T(8,128)(2,1)S(1)}) custom-call(bf16[192,4096]{1,0:T(8,128)(2,1)S(1)} %copy-done.7, bf16[192,924]{1,0:T(8,128)(2,1)S(1)} %copy-done.8, bf16[192,924]{1,0:T(8,128)(2,1)S(1)} %copy-done.9, bf16[192,924]{1,0:T(8,128)(2,1)S(1)} %copy-done.10, bf16[2,256,924]{2,1,0:T(8,128)(2,1)S(1)} %copy.15.w_hbm), custom_call_target="tpu_custom_call" | custom-call | flops 6000000000 | bytes 8000000 | tf_op jit(solution)/shard_map/pallas_call | solution.py:386
  116.0 0.0 copy-start.1
  116.0 1.3 copy-done.1
  117.3 0.0 copy-start.11
  117.3 0.0 copy-start.5
  117.3 0.0 copy-start.6
  117.3 2.5 %copy.16.mc = bf16[2,256,924]{2,1,0:T(8,128)(2,1)S(1)} copy(bf16[2,256,924]{1,0,2:T(2,128)(2,1)} %param.14) | data formatting | bytes 1892352 | tf_op args[5]
  119.8 0.0 copy-done.11
  119.9 1.9 %copy.17.sc = bf16[2,256,924]{2,1,0:T(8,128)(2,1)S(1)} copy(bf16[2,256,924]{1,0,2:T(2,128)(2,1)S(1)} %copy-done.11) | data formatting | bytes 1892352 | tf_op args[6]
  121.7 0.0 copy-done.5
  121.7 0.0 copy-done.6
  121.8 0.0 copy-start.2
  121.8 1.5 %copy-done.2 = f32[256,1920]{1,0:T(8,128)S(1)} copy-done((f32[256,1920]{1,0:T(8,128)S(1)}, f32[256,1920]{1,0:T(8,128)}, u32[]{:S(2)}) %copy-start.2) | copy-done | bytes 1966104
  123.3 3.1 %shard_map.137 = (f32[2,256,924]{2,1,0:T(8,128)S(1)}, bf16[2,256,924]{2,1,0:T(8,128)(2,1)S(1)}, bf16[2,256,924]{2,1,0:T(8,128)(2,1)S(1)}, f32[2,1,924]{2,1,0:T(1,128)}, f32[2,1,924]{2,1,0:T(1,128)}) custom-call(f32[256,1920]{1,0:T(8,128)S(1)} %copy-done.2, bf16[2,256,924]{2,1,0:T(8,128)(2,1)S(1)} %copy.16.mc, bf16[2,256,924]{2,1,0:T(8,128)(2,1)S(1)} %copy.17.sc, ...), custom_call_target="tpu_custom_call" | custom-call | tf_op jit(solution)/shard_map/pallas_call | solution.py:463
  126.4 0.0 copy-start
  126.4 1.3 copy-done
  127.7 0.0 copy-start.3
  127.7 1.0 copy-done.3
  128.7 0.0 copy-start.4
  128.7 4.1 %copy.18 = f32[2,256,924]{1,0,2:T(2,128)} copy(f32[2,256,924]{2,1,0:T(8,128)} %copy-done) | data formatting | bytes 3784704
  132.8 0.0 copy-done.4
  132.8 2.0 %copy.19 = bf16[2,256,924]{1,0,2:T(2,128)(2,1)} copy(bf16[2,256,924]{2,1,0:T(8,128)(2,1)S(1)} %copy-done.4) | data formatting | bytes 1892352
  134.8 2.0 %copy.20 = bf16[2,256,924]{1,0,2:T(2,128)(2,1)} copy(bf16[2,256,924]{2,1,0:T(8,128)(2,1)S(1)} %get-tuple-element.23) | data formatting | bytes 1892352
  136.8 0.6 copy.22
Async XLA Ops:
  0.6 2.6 %copy-start.8 = (bf16[192,924]{1,0:T(8,128)(2,1)S(1)}, bf16[192,924]{1,0:T(8,128)(2,1)}, u32[]{:S(2)}) copy-start(bf16[192,924]{1,0:T(8,128)(2,1)} %gate_hbm.1) | copy-start | bytes 1064452
  0.6 2.6 %copy-start.7 = (bf16[192,4096]{1,0:T(8,128)(2,1)S(1)}, bf16[192,4096]{1,0:T(8,128)(2,1)}, u32[]{:S(2)}) copy-start(bf16[192,4096]{1,0:T(8,128)(2,1)} %x_hbm.1) | copy-start | bytes 4718596
  3.3 1.0 copy-start.9
  4.3 1.0 copy-start.10
  116.0 1.3 copy-start.1
  117.3 2.5 %copy-start.11 = (bf16[2,256,924]{1,0,2:T(2,128)(2,1)S(1)}, bf16[2,256,924]{1,0,2:T(2,128)(2,1)}, u32[]{:S(2)}) copy-start(bf16[2,256,924]{1,0,2:T(2,128)(2,1)} %param.15) | copy-start | bytes 2838532
  117.3 4.4 %copy-start.5 = (f32[2,1,924]{2,1,0:T(1,128)S(1)}, f32[2,1,924]{2,1,0:T(1,128)}, u32[]{:S(2)}) copy-start(f32[2,1,924]{2,1,0:T(1,128)} %ms.1) | copy-start | bytes 22180
  117.3 4.4 %copy-start.6 = (f32[2,1,924]{2,1,0:T(1,128)S(1)}, f32[2,1,924]{2,1,0:T(1,128)}, u32[]{:S(2)}) copy-start(f32[2,1,924]{2,1,0:T(1,128)} %ss.1) | copy-start | bytes 22180
  121.8 1.5 %copy-start.2 = (f32[256,1920]{1,0:T(8,128)S(1)}, f32[256,1920]{1,0:T(8,128)}, u32[]{:S(2)}) copy-start(f32[256,1920]{1,0:T(8,128)} %copy-done.1) | copy-start | bytes 5898244
  126.4 1.3 copy-start
  127.7 1.0 copy-start.3
  128.7 4.1 %copy-start.4 = (bf16[2,256,924]{2,1,0:T(8,128)(2,1)S(1)}, bf16[2,256,924]{2,1,0:T(8,128)(2,1)}, u32[]{:S(2)}) copy-start(bf16[2,256,924]{2,1,0:T(8,128)(2,1)} %copy-done.3) | copy-start | bytes 2838532

commit v2 on v1

v2 whole, which is shorter than its diff:
```python
import functools

import jax
import jax.numpy as jnp
from jax import lax
from jax.experimental import pallas as pl
from jax.experimental.pallas import tpu as pltpu
from jax.sharding import PartitionSpec as P

MESH = pl.DeviceIdType.MESH
F32 = jnp.float32
BF16 = jnp.bfloat16

beta_first = 0.9
beta_second = 0.95
bias_first = 0.19
bias_second = 0.0975
adam_eps = 1e-08
scale_eps = 1e-06

TOK = 192
HALF = 96
ROWS = 256
HID = 924
PACK = 1920
NZ = 8
NM = 8
NY = 4
TOKENS = 3072
QR = 48
LANE = 128

GROUPS = ((0, 384, 0), (384, 384, 768), (768, 128, 1536))
TAIL_AT = 1792
TAIL_FROM = 896
TAIL = HID - TAIL_FROM
CHUNKS = tuple((start, 384) for start in range(0, PACK, 384))
A, B, C, D, E = range(5)
VIEW = 4 * HID
VIEW_PAD = 4 * 960


OUTS = (
    jax.ShapeDtypeStruct((TOK, 256), BF16),
    jax.ShapeDtypeStruct((VIEW, LANE), F32),
    jax.ShapeDtypeStruct((VIEW, LANE), BF16),
    jax.ShapeDtypeStruct((VIEW, LANE), BF16),
    jax.ShapeDtypeStruct((2, 1, HID), F32),
    jax.ShapeDtypeStruct((2, 1, HID), F32),
)


def slot_of(rel):
    rel = rel % NZ
    if rel == 0:
        return 0
    if rel == 4:
        return 7
    return 2 * rel if rel < 4 else 2 * (NZ - rel) - 1


REL_OF = {slot_of(rel): rel for rel in range(NZ)}
ROUNDS = ((0, 1), (1, 3), (3, 5), (5, 7), (7, 8))


def pack_tail(first, second):
    rows = first.shape[0]
    blank = jnp.zeros((rows, 64 - TAIL), first.dtype)
    return jnp.concatenate([first, blank, second, blank], axis=1)


def comm_kernel(
    x_hbm, gate_hbm, up_hbm, gh_hbm, w_hbm, mc_hbm, sc_hbm, ms_hbm, ss_hbm,
    ig_out, step_out, mc_out, sc_out, ms_out, ss_out,
    gate_v, up_v, gh_v, w_v, w_f, mc_v, sc_v, ms_v, ss_v, ms_n, ss_n, m_f, s_f, step_v,
    gbuf, xbuf, xt, wt, dw_send, dw_recv, dw_own, c_send, c_recv, keep, rs_src, rs_recv, f_src, f_here, f_buf, out_v,
    load_sem, ring_s, ring_r, x1_s, x1_r, x2_s, x2_r, x3_s, x3_r, w_s, w_r,
    dw_s, dw_r, core_s, core_r, rs_s, rs_r, fz_s, fz_r, fin_s, fin_r, out_sem,
):
    d = lax.axis_index("dp")
    t = lax.axis_index("tensor")
    z, xl = d // 2, d % 2
    m, c = t // 2, t % 2
    y, xh = m % 4, m // 4

    def at_z(r):
        return (((z + r) % NZ) * 2 + xl, t)

    def at_y(e):
        return (d, (xh * 4 + (y + e) % NY) * 2 + c)

    def at_m(chip):
        return (d, (chip % NM) * 2 + c)

    sibling = (d, m * 2 + (1 - c))
    partner = (z * 2 + (1 - xl), t)

    loads = [
        pltpu.make_async_copy(gate_hbm, gate_v, load_sem.at[0]),
        pltpu.make_async_copy(up_hbm, up_v, load_sem.at[1]),
        pltpu.make_async_copy(gh_hbm, gh_v, load_sem.at[2]),
        pltpu.make_async_copy(w_hbm, w_v, load_sem.at[3]),
        pltpu.make_async_copy(mc_hbm, mc_v, load_sem.at[4]),
        pltpu.make_async_copy(sc_hbm, sc_v, load_sem.at[5]),
        pltpu.make_async_copy(ms_hbm, ms_v, load_sem.at[6]),
        pltpu.make_async_copy(ss_hbm, ss_v, load_sem.at[7]),
    ]
    for load in loads[:3]:
        load.start()

    barrier = pltpu.get_barrier_semaphore()
    for r in range(1, NZ):
        pl.semaphore_signal(barrier, inc=1, device_id=at_z(r), device_id_type=MESH)
    for e in range(1, NM):
        pl.semaphore_signal(barrier, inc=1, device_id=at_m(m + e), device_id_type=MESH)
    pl.semaphore_signal(barrier, inc=1, device_id=sibling, device_id_type=MESH)
    pl.semaphore_signal(barrier, inc=1, device_id=partner, device_id_type=MESH)

    sends = []

    def remote(src, dst, send_sem, recv_sem, where):
        return pltpu.make_async_remote_copy(
            src_ref=src, dst_ref=dst, send_sem=send_sem, recv_sem=recv_sem,
            device_id=where, device_id_type=MESH,
        )

    def launch(copy):
        copy.start()
        sends.append(copy)
        return copy

    def grads(first, width):
        g = gate_v[:, first:first + width].astype(F32)
        u = up_v[:, first:first + width].astype(F32)
        h = gh_v[:, first:first + width].astype(F32)
        sig = jax.nn.sigmoid(g)
        g_up = (h * g * sig).astype(BF16)
        g_gate = (h * u * sig * (1.0 + g * (1.0 - sig))).astype(BF16)
        return g_gate, g_up

    def fill(k):
        first, width, at = GROUPS[k]
        g_gate, g_up = grads(first, width)
        gbuf[0, :, at:at + width] = g_gate
        gbuf[0, :, at + width:at + 2 * width] = g_up

    def fill_tail():
        g_gate, g_up = grads(TAIL_FROM, TAIL)
        gbuf[0, :, TAIL_AT:TAIL_AT + LANE] = pack_tail(g_gate, g_up)

    ring = {}
    for k, (start, width) in enumerate(CHUNKS):
        for s in range(1, 5):
            for way in range(2):
                for h in range(2):
                    if s == 4 and way != h:
                        continue
                    sign = -1 if way == 0 else 1
                    src_slot, dst_slot = slot_of(sign * (s - 1)), slot_of(sign * s)
                    rows, columns = pl.ds(h * HALF, HALF), pl.ds(start, width)
                    ring[k, s, way, h] = remote(
                        gbuf.at[src_slot, rows, columns],
                        gbuf.at[dst_slot, rows, columns],
                        ring_s.at[k, s - 1, way, h], ring_r.at[k, s - 1, way, h],
                        at_z(1 if way == 0 else -1),
                    )

    def step(k, s):
        for h in range(2):
            for way in range(2):
                if (k, s, way, h) in ring:
                    if s > 1:
                        ring[k, s - 1, way, h].wait_recv()
                    launch(ring[k, s, way, h])

    def third(k):
        for way in range(2):
            ring[k, 3, way, 1 - way].wait_recv()

    def fourth(k):
        for way in range(2):
            ring[k, 4, way, way].wait_recv()

    q_at = pl.multiple_of(y * QR, 16)
    core_half = pl.ds(pl.multiple_of(c * 256, 256), 256)

    def x_columns(r):
        return pl.ds(pl.multiple_of(((z + r) % NZ) * 512 + c * 256, 256), 256)

    x_first = []
    x_own = pltpu.make_async_copy(
        x_hbm.at[pl.ds(q_at, QR), x_columns(0)],
        xbuf.at[0, pl.ds(q_at, QR), core_half], x1_r.at[0],
    )

    def x_start():
        x_own.start()
        for r in range(1, NZ):
            x_first.append(launch(remote(
                x_hbm.at[pl.ds(q_at, QR), x_columns(r)],
                xbuf.at[slot_of(-r), pl.ds(q_at, QR), core_half],
                x1_s.at[r], x1_r.at[r], at_z(r),
            )))

    def x_second():
        x_own.wait()
        for copy in x_first:
            copy.wait_recv()
        piece = xbuf.at[:, pl.ds(q_at, QR), core_half]
        for e in range(1, NY):
            launch(remote(piece, piece, x2_s.at[e], x2_r.at[e], at_y(e)))

    def x_third():
        for e in range(1, NY):
            rows = pl.ds(pl.multiple_of(((y + NY - e) % NY) * QR, 16), QR)
            there = xbuf.at[:, rows, core_half]
            remote(there, there, x2_s.at[e], x2_r.at[e], at_y(e)).wait_recv()
        mine = xbuf.at[:, :, core_half]
        launch(remote(mine, mine, x3_s, x3_r, sibling))

    def x_turn():
        theirs = xbuf.at[:, :, pl.ds(pl.multiple_of((1 - c) * 256, 256), 256)]
        remote(theirs, theirs, x3_s, x3_r, sibling).wait_recv()
        for j in range(2):
            for i in range(4):
                block = xbuf[2 * i:2 * i + 2, :, j * 256:(j + 1) * 256].reshape(2 * TOK, 256)
                xt[j, :, i * 2 * TOK:(i + 1) * 2 * TOK] = block.T

    mine_w = wt.at[xl]
    w_copy = remote(mine_w, mine_w, w_s, w_r, partner)

    def w_prepare():
        loads[3].wait()
        w_f[:VIEW, :] = w_v[...].astype(F32)
        w_f[VIEW:, :] = jnp.zeros((VIEW_PAD - VIEW, LANE), F32)
        for p in range(2):
            for tile in range(2):
                lanes = slice(tile * LANE, (tile + 1) * LANE)
                for first, width, at in GROUPS + ((TAIL_FROM, 64, TAIL_AT),):
                    piece = w_f[pl.ds(first * 4 + tile * 2 + p, width, stride=4), :]
                    wt[xl, at + p * width:at + (p + 1) * width, lanes] = piece.astype(BF16)
        launch(w_copy)

    def w_wait():
        theirs = wt.at[1 - xl]
        remote(theirs, theirs, w_s, w_r, partner).wait_recv()

    dw_copies = {}

    def dw_product(j, k):
        start, width = CHUNKS[k]
        block = gbuf[:, :, start:start + width].reshape(NZ * TOK, width)
        return jnp.dot(xt[j], block, preferred_element_type=F32)

    def dw_out(k):
        start, width = CHUNKS[k]
        dw_send[:, start:start + width] = dw_product(1 - xl, k).astype(BF16)
        columns = pl.ds(start, width)
        dw_copies[k] = launch(remote(
            dw_send.at[:, columns], dw_recv.at[:, columns], dw_s.at[k], dw_r.at[k], partner
        ))

    def dw_keep(k):
        start, width = CHUNKS[k]
        dw_own[:, start:start + width] = dw_product(xl, k)

    out_copies = []

    def codes_prepare():
        for load in loads[4:]:
            load.wait()
        m_f[:VIEW, :] = mc_v[...].astype(F32)
        s_f[:VIEW, :] = sc_v[...].astype(F32)
        m_f[VIEW:, :] = jnp.zeros((VIEW_PAD - VIEW, LANE), F32)
        s_f[VIEW:, :] = jnp.zeros((VIEW_PAD - VIEW, LANE), F32)

    def column(ref, hidden, p):
        if hidden == TAIL_FROM:
            blank = jnp.ones((1, LANE - TAIL), F32)
            row = jnp.concatenate([ref[p, :, TAIL_FROM:HID], blank], axis=1)
        else:
            row = ref[p, :, hidden:hidden + LANE]
        return jnp.broadcast_to(row, (LANE, LANE)).T

    def top(parts):
        largest = jnp.maximum(jnp.abs(parts[0]), jnp.abs(parts[1]))
        largest = jnp.max(largest, axis=1, keepdims=True) + scale_eps
        return jnp.broadcast_to(largest, parts[0].shape)

    def adam(grads_by_tile, hidden, p):
        count = grads_by_tile[0].shape[0]
        m_scale = beta_first * column(ms_v, hidden, p)[:count]
        s_scale = beta_second * column(ss_v, hidden, p)[:count]
        places = [pl.ds(hidden * 4 + tile * 2 + p, count, stride=4) for tile in range(2)]
        moments, seconds = [], []
        for place, grad in zip(places, grads_by_tile):
            moment = m_f[place, :] * m_scale + (1.0 - beta_first) * grad
            second = s_f[place, :] * s_scale + (1.0 - beta_second) * grad * grad
            scale = jnp.sqrt(second * (1.0 / bias_second)) + adam_eps
            step_v[place, :] = moment * (1.0 / bias_first) / scale
            moments.append(moment)
            seconds.append(second)
        for values, store, new in ((moments, m_f, ms_n), (seconds, s_f, ss_n)):
            largest = top(values)
            if count < LANE:
                new[p, :, TAIL_FROM:HID] = largest.T[:1, :TAIL]
            else:
                new[p, :, hidden:hidden + LANE] = largest.T[:1]
            inverse = 1.0 / largest
            for place, value in zip(places, values):
                store[place, :] = value * inverse

    def dw_end(k):
        dw_copies[k].wait_recv()
        start, width = CHUNKS[k]
        for at in range(start, start + width, LANE):
            columns = slice(at, at + LANE)
            total = (dw_own[:, columns] + dw_recv[:, columns].astype(F32)) * (1.0 / TOKENS)
            total = total.T
            if at == TAIL_AT:
                places = ((0, 64, TAIL_FROM, 0), (64, 64, TAIL_FROM, 1))
            else:
                first, size, begin = [g for g in GROUPS if g[2] <= at][-1]
                p, inner = (at - begin) // size, (at - begin) % size
                places = ((0, LANE, first + inner, p),)
            for lo, count, hidden, p in places:
                adam([total[lo:lo + count, :LANE], total[lo:lo + count, LANE:]], hidden, p)

    def adam_out(i):
        lo, hi = ((0, 1536), (1536, 3072), (3072, VIEW))[i]
        mc_v[lo:hi, :] = m_f[lo:hi, :].astype(BF16)
        sc_v[lo:hi, :] = s_f[lo:hi, :].astype(BF16)
        rows = pl.ds(lo, hi - lo)
        pairs = [(step_v, step_out), (mc_v, mc_out), (sc_v, sc_out)]
        copies = [
            pltpu.make_async_copy(src.at[rows], dst.at[rows], out_sem.at[i, q])
            for q, (src, dst) in enumerate(pairs)
        ]
        if i == 2:
            copies.append(pltpu.make_async_copy(ms_n, ms_out, out_sem.at[i, 3]))
            copies.append(pltpu.make_async_copy(ss_n, ss_out, out_sem.at[i, 4]))
        for copy in copies:
            copy.start()
        out_copies.extend(copies)

    core_copies = {}
    rs_copies = {}

    def dx_away(n):
        lo, hi = ROUNDS[n]
        block = gbuf[lo:hi].reshape((hi - lo) * TOK, PACK)
        there = jnp.dot(block, wt[1 - c], preferred_element_type=F32).astype(BF16)
        c_send[lo:hi] = there.reshape(hi - lo, TOK, 256)
        core_copies[n] = launch(remote(
            c_send.at[lo:hi], c_recv.at[lo:hi], core_s.at[n], core_r.at[n], sibling
        ))

    def dx_keep(n):
        lo, hi = ROUNDS[n]
        block = gbuf[lo:hi].reshape((hi - lo) * TOK, PACK)
        keep[lo:hi] = jnp.dot(block, wt[c], preferred_element_type=F32).reshape(hi - lo, TOK, 256)

    def dx_scatter(n):
        lo, hi = ROUNDS[n]
        core_copies[n].wait_recv()
        rs_src[lo:hi] = (keep[lo:hi] + c_recv[lo:hi].astype(F32)).astype(BF16)
        for e in range(1, NY):
            to = pl.ds(pl.multiple_of(((y + e) % NY) * QR, 16), QR)
            rs_copies[n, e] = launch(remote(
                rs_src.at[lo:hi, to], rs_recv.at[e, lo:hi], rs_s.at[n, e], rs_r.at[n, e], at_y(e)
            ))

    def dx_finish(n):
        lo, hi = ROUNDS[n]
        for e in range(1, NY):
            rs_copies[n, e].wait_recv()
        total = rs_src[lo:hi, pl.ds(q_at, QR)].astype(F32)
        for e in range(1, NY):
            total = total + rs_recv[e, lo:hi].astype(F32)
        if lo == 0:
            f_here[0:1] = total.astype(BF16)
            return
        f_src[lo:hi] = total.astype(BF16)
        for p in range(lo, hi):
            q = slot_of(-REL_OF[p])
            launch(remote(f_src.at[p], f_here.at[q], fz_s.at[q], fz_r.at[q], at_z(REL_OF[p])))

    home_copies = []

    def dx_home(n):
        for p in range(*ROUNDS[n]):
            rel = REL_OF[p]
            if p:
                there = f_here.at[p]
                remote(there, there, fz_s.at[p], fz_r.at[p], at_z(1)).wait_recv()
            chip = (z + rel) % NM
            target = f_buf.at[xh, pl.ds(q_at, QR)]
            away = remote(f_here.at[p], target, fin_s.at[p], fin_r, at_m(chip))
            local = pltpu.make_async_copy(f_here.at[p], target, fin_r)
            here = chip == m
            pl.when(here)(local.start)
            pl.when(jnp.logical_not(here))(away.start)
            home_copies.append((here, away))

    for load in loads[:3]:
        load.wait()
    fill(0)
    pl.semaphore_wait(barrier, (NZ - 1) + (NM - 1) + 2)

    step(A, 1)
    x_start()
    step(B, 1)
    for load in loads[3:]:
        load.start()
    fill(1)
    fill(2)
    fill_tail()
    step(A, 2)
    w_prepare()
    step(B, 2)
    x_second()
    step(A, 3)
    step(C, 1)
    codes_prepare()
    step(A, 4)
    x_third()
    step(B, 3)
    x_turn()
    step(C, 2)
    third(A)
    fourth(A)
    dw_out(A)
    dw_keep(A)
    step(B, 4)
    step(D, 1)
    step(C, 3)
    third(B)
    fourth(B)
    dw_out(B)
    dw_keep(B)
    step(D, 2)
    dw_end(A)
    step(C, 4)
    w_wait()
    dx_away(0)
    step(E, 1)
    dx_keep(0)
    step(D, 3)
    third(C)
    fourth(C)
    dw_out(C)
    dw_keep(C)
    dx_scatter(0)
    step(E, 2)
    dx_away(1)
    dx_keep(1)
    step(D, 4)
    dx_scatter(1)
    dw_end(B)
    adam_out(0)
    dx_finish(0)
    step(E, 3)
    dx_home(0)
    dx_away(2)
    dx_keep(2)
    dx_scatter(2)
    dx_finish(1)
    third(D)
    fourth(D)
    dw_out(D)
    step(E, 4)
    dw_keep(D)
    third(E)
    dx_away(3)
    dx_keep(3)
    dx_scatter(3)
    fourth(E)
    dx_away(4)
    dw_out(E)
    dx_keep(4)
    dx_scatter(4)
    dx_finish(2)
    dw_keep(E)
    dx_home(1)
    dx_finish(3)
    dw_end(C)
    dx_finish(4)
    dx_home(2)
    dw_end(D)
    adam_out(1)
    dx_home(3)
    dx_home(4)
    dw_end(E)
    adam_out(2)

    pltpu.make_async_copy(f_buf, f_buf, fin_r).wait()
    out_v[...] = (f_buf[0].astype(F32) + f_buf[1].astype(F32)).astype(BF16)
    result = pltpu.make_async_copy(out_v, ig_out, out_sem.at[0, 3])
    result.start()
    for copy in sends:
        copy.wait_send()
    for here, away in home_copies:
        pl.when(jnp.logical_not(here))(away.wait_send)
    for copy in out_copies:
        copy.wait()
    result.wait()


def compute(*operands):
    hbm = pl.BlockSpec(memory_space=pltpu.HBM)
    dma = pltpu.SemaphoreType.DMA
    n = len(CHUNKS)
    return pl.pallas_call(
        comm_kernel,
        out_shape=OUTS,
        in_specs=[hbm] * 9,
        out_specs=[pl.BlockSpec(memory_space=pl.ANY)] * 6,
        scratch_shapes=[
            pltpu.VMEM((TOK, HID), BF16),
            pltpu.VMEM((TOK, HID), BF16),
            pltpu.VMEM((TOK, HID), BF16),
            pltpu.VMEM((VIEW, LANE), BF16),
            pltpu.VMEM((VIEW_PAD, LANE), F32),
            pltpu.VMEM((VIEW, LANE), BF16),
            pltpu.VMEM((VIEW, LANE), BF16),
            pltpu.VMEM((2, 1, HID), F32),
            pltpu.VMEM((2, 1, HID), F32),
            pltpu.VMEM((2, 1, HID), F32),
            pltpu.VMEM((2, 1, HID), F32),
            pltpu.VMEM((VIEW_PAD, LANE), F32),
            pltpu.VMEM((VIEW_PAD, LANE), F32),
            pltpu.VMEM((VIEW_PAD, LANE), F32),
            pltpu.VMEM((NZ, TOK, PACK), BF16),
            pltpu.VMEM((NZ, TOK, 512), BF16),
            pltpu.VMEM((2, 256, NZ * TOK), BF16),
            pltpu.VMEM((2, PACK, 256), BF16),
            pltpu.VMEM((ROWS, PACK), BF16),
            pltpu.VMEM((ROWS, PACK), BF16),
            pltpu.VMEM((ROWS, PACK), F32),
            pltpu.VMEM((NZ, TOK, 256), BF16),
            pltpu.VMEM((NZ, TOK, 256), BF16),
            pltpu.VMEM((NZ, TOK, 256), F32),
            pltpu.VMEM((NZ, TOK, 256), BF16),
            pltpu.VMEM((NY, NZ, QR, 256), BF16),
            pltpu.VMEM((NZ, QR, 256), BF16),
            pltpu.VMEM((NZ, QR, 256), BF16),
            pltpu.VMEM((2, TOK, 256), BF16),
            pltpu.VMEM((TOK, 256), BF16),
            dma((8,)),
            dma((n, 4, 2, 2)), dma((n, 4, 2, 2)),
            dma((NZ,)), dma((NZ,)),
            dma((NY,)), dma((NY,)),
            dma, dma, dma, dma,
            dma((n,)), dma((n,)),
            dma((5,)), dma((5,)),
            dma((5, NY)), dma((5, NY)),
            dma((NZ,)), dma((NZ,)),
            dma((NZ,)), dma,
            dma((3, 5)),
        ],
        compiler_params=pltpu.CompilerParams(
            collective_id=0, has_side_effects=True, vmem_limit_bytes=60 * 1024 * 1024
        ),
        cost_estimate=pl.CostEstimate(
            flops=6_000_000_000, bytes_accessed=12_000_000, transcendentals=700_000
        ),
    )(*operands)


PIECES = tuple(
    (which, lo, min(lo + 1232, VIEW)) for lo in range(0, VIEW, 1232) for which in (1, 2, 3)
) + ((0, 0, TOK), (4, 0, 2), (5, 0, 2))


def place_kernel(*refs):
    sources, results, held, sem = refs[:6], refs[6:12], refs[12:18], refs[18]

    def moves(n, first, second):
        which, lo, hi = PIECES[n]
        rows = pl.ds(lo, hi - lo)
        return pltpu.make_async_copy(first[which].at[rows], second[which].at[rows], sem.at[n])

    arrivals = [moves(n, sources, held) for n in range(len(PIECES))]
    for copy in arrivals:
        copy.start()
    departures = []
    for n, copy in enumerate(arrivals):
        copy.wait()
        departures.append(moves(n, held, results))
        departures[-1].start()
    for copy in departures:
        copy.wait()


def place(*results):
    hbm = pl.BlockSpec(memory_space=pltpu.HBM)
    return pl.pallas_call(
        place_kernel,
        out_shape=OUTS,
        in_specs=[hbm] * 6,
        out_specs=[hbm] * 6,
        scratch_shapes=[pltpu.VMEM(out.shape, out.dtype) for out in OUTS]
        + [pltpu.SemaphoreType.DMA((len(PIECES),))],
        compiler_params=pltpu.CompilerParams(vmem_limit_bytes=60 * 1024 * 1024),
    )(*results)


def view(a):
    a = a.transpose(2, 0, 1).reshape(HID, 2, 2, LANE)
    return a.transpose(0, 2, 1, 3).reshape(VIEW, LANE)


def unview(a):
    a = a.reshape(HID, 2, 2, LANE).transpose(0, 2, 1, 3)
    return a.reshape(HID, 2, ROWS).transpose(1, 2, 0)


def per_device(x, gate, up, gh, w, mc, sc, ms, ss):
    results = compute(x, gate, up, gh, view(w), view(mc), view(sc), ms, ss)
    ig, step, mc_new, sc_new, ms_new, ss_new = place(*results)
    return ig, unview(step), unview(mc_new), unview(sc_new), ms_new, ss_new


def solution(mesh):
    whole = P(None, "dp", "tensor")
    token = P("dp", "tensor")
    return jax.shard_map(
        per_device,
        mesh=mesh,
        in_specs=(P("dp", None), token, token, token, whole, whole, whole, whole, whole),
        out_specs=(token, whole, whole, whole, whole, whole),
        check_vma=False,
    )
```

time: 138 us -> 95.6 us (0.69)
  local copies, waits for them, and re-layouts: 22.9 us -> 0 us
  Pallas kernels: 114 us -> 94.7 us
    unnamed x31 -> x0, local copies, waits for them, and re-layouts: 22.9 us -> none
    pallas_call x2, Pallas kernels: 114 us -> 94.7 us  [the longest x1 91.6 us: compute(): pl.pallas_call(comm_kernel, out_shape=OUTS, in_specs=[hbm] * 9, out_specs...]
where the time goes in v2:
time: 95.6 us; the launch traced here: 95.5 us
  Pallas kernels  94.7 us (99%)
    pallas_call x1, Pallas kernels, compute(): pl.pallas_call(comm_kernel, out_shape=OUTS, in_specs=[hbm] * 9, out_specs...  91.6 us
    pallas_call x1, Pallas kernels, place(): pl.pallas_call(place_kernel, out_shape=OUTS, in_specs=[hbm] * 6, out_spec...  3.08 us

profile of v2, /device:TPU:6, one launch (start us, length us, event | category | flops | bytes accessed | tf_op | source)
XLA Modules:
  0.0 95.5 jit_solution(8709318139869214897)
XLA Ops:
  0.6 91.6 %shard_map.136 = (bf16[192,256]{1,0:T(8,128)(2,1)}, f32[3696,128]{1,0:T(8,128)}, bf16[3696,128]{1,0:T(8,128)(2,1)}, bf16[3696,128]{1,0:T(8,128)(2,1)}, f32[2,1,924]{2,1,0:T(1,128)}, /*index=5*/f32[2,1,924]{2,1,0:T(1,128)}) custom-call(bf16[192,4096]{1,0:T(8,128)(2,1)} %x_hbm.1, bf16[192,924]{1,0:T(8,128)(2,1)} %gate_hbm.1, bf16[192,924]{1,0:T(8,128)(2,1)} %up_hbm.1, ...), custom_call_target="tpu_custom_call" | custom-call | flops 6000000000 | bytes 12000000 | tf_op jit(solution)/shard_map/pallas_call | solution.py:513
  92.2 3.1 %shard_map.137 = (bf16[192,256]{1,0:T(8,128)(2,1)}, f32[3696,128]{1,0:T(8,128)}, bf16[3696,128]{1,0:T(8,128)(2,1)}, bf16[3696,128]{1,0:T(8,128)(2,1)}, f32[2,1,924]{2,1,0:T(1,128)}, /*index=5*/f32[2,1,924]{2,1,0:T(1,128)}) custom-call(bf16[192,256]{1,0:T(8,128)(2,1)} %get-tuple-element.18.refs_0_, f32[3696,128]{1,0:T(8,128)} %get-tuple-element.19.refs_1_, ...), custom_call_target="tpu_custom_call" | custom-call | tf_op jit(solution)/shard_map/pallas_call | solution.py:597

commit v3 on v2

--- a/solution.py
+++ b/solution.py
@@ -34,6 +34,7 @@
 TAIL_AT = 1792
 TAIL_FROM = 896
 TAIL = HID - TAIL_FROM
+FOLD = 640
 CHUNKS = tuple((start, 384) for start in range(0, PACK, 384))
 A, B, C, D, E = range(5)
 VIEW = 4 * HID
@@ -73,9 +74,10 @@
     x_hbm, gate_hbm, up_hbm, gh_hbm, w_hbm, mc_hbm, sc_hbm, ms_hbm, ss_hbm,
     ig_out, step_out, mc_out, sc_out, ms_out, ss_out,
     gate_v, up_v, gh_v, w_v, w_f, mc_v, sc_v, ms_v, ss_v, ms_n, ss_n, m_f, s_f, step_v,
-    gbuf, xbuf, xt, wt, dw_send, dw_recv, dw_own, c_send, c_recv, keep, rs_src, rs_recv, f_src, f_here, f_buf, out_v,
+    gbuf, fold, xbuf, xt, wt, dw_send, dw_recv, dw_own, c_send, c_recv, keep, rs_src, rs_recv, f_src, f_here, f_buf, out_v,
     load_sem, ring_s, ring_r, x1_s, x1_r, x2_s, x2_r, x3_s, x3_r, w_s, w_r,
     dw_s, dw_r, core_s, core_r, rs_s, rs_r, fz_s, fz_r, fin_s, fin_r, out_sem,
+    z_near, z_far, y_near, plane_in,
 ):
     d = lax.axis_index("dp")
     t = lax.axis_index("tensor")
@@ -84,10 +86,10 @@
     y, xh = m % 4, m // 4
 
     def at_z(r):
-        return (((z + r) % NZ) * 2 + xl, t)
+        return (((z + r + NZ) % NZ) * 2 + xl, t)
 
     def at_y(e):
-        return (d, (xh * 4 + (y + e) % NY) * 2 + c)
+        return (d, (xh * 4 + (y + e + NY) % NY) * 2 + c)
 
     def at_m(chip):
         return (d, (chip % NM) * 2 + c)
@@ -108,13 +110,13 @@
     for load in loads[:3]:
         load.start()
 
+    def tell(sem, devices):
+        for device in devices:
+            pl.semaphore_signal(sem, inc=1, device_id=device, device_id_type=MESH)
+
     barrier = pltpu.get_barrier_semaphore()
-    for r in range(1, NZ):
-        pl.semaphore_signal(barrier, inc=1, device_id=at_z(r), device_id_type=MESH)
-    for e in range(1, NM):
-        pl.semaphore_signal(barrier, inc=1, device_id=at_m(m + e), device_id_type=MESH)
-    pl.semaphore_signal(barrier, inc=1, device_id=sibling, device_id_type=MESH)
-    pl.semaphore_signal(barrier, inc=1, device_id=partner, device_id_type=MESH)
+    near = [at_z(1), at_z(-1), at_y(1), at_y(-1), at_m(m + 4), sibling, partner]
+    tell(barrier, near)
 
     sends = []
 
@@ -147,6 +149,29 @@
     def fill_tail():
         g_gate, g_up = grads(TAIL_FROM, TAIL)
         gbuf[0, :, TAIL_AT:TAIL_AT + LANE] = pack_tail(g_gate, g_up)
+
+    fold_at = CHUNKS[E][0]
+
+    def fold_own():
+        for half in range(2):
+            rows = slice(half * HALF, (half + 1) * HALF)
+            fold[0, :, half * 256:(half + 1) * 256] = gbuf[0, rows, fold_at:fold_at + 256]
+        first, second = (
+            gbuf[0, half * HALF:(half + 1) * HALF, TAIL_AT:TAIL_AT + LANE].astype(F32)
+            for half in range(2)
+        )
+        fold[0, :, 512:FOLD] = (first + pltpu.roll(second, 32, 1)).astype(BF16)
+
+    def unfold(n):
+        lane = lax.broadcasted_iota(jnp.int32, (HALF, LANE), 1)
+        kept = lane % 64 < TAIL
+        for slot in range(*ROUNDS[n]):
+            tails = fold[slot, :, 512:FOLD].astype(F32)
+            for half in range(2):
+                rows = slice(half * HALF, (half + 1) * HALF)
+                gbuf[slot, rows, fold_at:fold_at + 256] = fold[slot, :, half * 256:(half + 1) * 256]
+                tail = tails if half == 0 else pltpu.roll(tails, 96, 1)
+                gbuf[slot, rows, TAIL_AT:TAIL_AT + LANE] = jnp.where(kept, tail, 0.0).astype(BF16)
 
     ring = {}
     for k, (start, width) in enumerate(CHUNKS):
@@ -158,16 +183,21 @@
                     sign = -1 if way == 0 else 1
                     src_slot, dst_slot = slot_of(sign * (s - 1)), slot_of(sign * s)
                     rows, columns = pl.ds(h * HALF, HALF), pl.ds(start, width)
+                    source, target = (gbuf.at[i, rows, columns] for i in (src_slot, dst_slot))
+                    if k == E:
+                        rows = pl.ds(h * QR, QR)
+                        source, target = fold.at[src_slot, rows], fold.at[dst_slot, rows]
                     ring[k, s, way, h] = remote(
-                        gbuf.at[src_slot, rows, columns],
-                        gbuf.at[dst_slot, rows, columns],
+                        source,
+                        target,
                         ring_s.at[k, s - 1, way, h], ring_r.at[k, s - 1, way, h],
                         at_z(1 if way == 0 else -1),
                     )
 
     def step(k, s):
-        for h in range(2):
+        for turn in range(2):
             for way in range(2):
+                h = turn if way == 0 else 1 - turn
                 if (k, s, way, h) in ring:
                     if s > 1:
                         ring[k, s - 1, way, h].wait_recv()
@@ -405,40 +435,48 @@
     for load in loads[:3]:
         load.wait()
     fill(0)
-    pl.semaphore_wait(barrier, (NZ - 1) + (NM - 1) + 2)
+    pl.semaphore_wait(barrier, len(near))
 
     step(A, 1)
-    x_start()
+    tell(z_near, [at_z(1), at_z(-1)])
+    tell(y_near, [at_y(1), at_y(-1)])
     step(B, 1)
     for load in loads[3:]:
         load.start()
     fill(1)
     fill(2)
     fill_tail()
+    fold_own()
+    pl.semaphore_wait(z_near, 2)
+    tell(z_far, [at_z(2), at_z(-2)])
+    pl.semaphore_wait(y_near, 2)
+    tell(plane_in, [at_m(m + 4)])
     step(A, 2)
     w_prepare()
+    pl.semaphore_wait(z_far, 2)
+    x_start()
     step(B, 2)
-    x_second()
+    codes_prepare()
     step(A, 3)
     step(C, 1)
-    codes_prepare()
+    x_second()
     step(A, 4)
+    step(B, 3)
+    step(C, 2)
+    step(B, 4)
+    step(D, 1)
     x_third()
-    step(B, 3)
+    step(C, 3)
     x_turn()
-    step(C, 2)
     third(A)
     fourth(A)
     dw_out(A)
     dw_keep(A)
-    step(B, 4)
-    step(D, 1)
-    step(C, 3)
     third(B)
     fourth(B)
     dw_out(B)
+    step(D, 2)
     dw_keep(B)
-    step(D, 2)
     dw_end(A)
     step(C, 4)
     w_wait()
@@ -452,6 +490,7 @@
     dw_keep(C)
     dx_scatter(0)
     step(E, 2)
+    unfold(1)
     dx_away(1)
     dx_keep(1)
     step(D, 4)
@@ -460,7 +499,9 @@
     adam_out(0)
     dx_finish(0)
     step(E, 3)
+    pl.semaphore_wait(plane_in, 1)
     dx_home(0)
+    unfold(2)
     dx_away(2)
     dx_keep(2)
     dx_scatter(2)
@@ -471,10 +512,12 @@
     step(E, 4)
     dw_keep(D)
     third(E)
+    unfold(3)
     dx_away(3)
     dx_keep(3)
     dx_scatter(3)
     fourth(E)
+    unfold(4)
     dx_away(4)
     dw_out(E)
     dx_keep(4)
@@ -509,6 +552,7 @@
 def compute(*operands):
     hbm = pl.BlockSpec(memory_space=pltpu.HBM)
     dma = pltpu.SemaphoreType.DMA
+    regular = pltpu.SemaphoreType.REGULAR
     n = len(CHUNKS)
     return pl.pallas_call(
         comm_kernel,
@@ -531,6 +575,7 @@
             pltpu.VMEM((VIEW_PAD, LANE), F32),
             pltpu.VMEM((VIEW_PAD, LANE), F32),
             pltpu.VMEM((NZ, TOK, PACK), BF16),
+            pltpu.VMEM((NZ, HALF, FOLD), BF16),
             pltpu.VMEM((NZ, TOK, 512), BF16),
             pltpu.VMEM((2, 256, NZ * TOK), BF16),
             pltpu.VMEM((2, PACK, 256), BF16),
@@ -557,6 +602,7 @@
             dma((NZ,)), dma((NZ,)),
             dma((NZ,)), dma,
             dma((3, 5)),
+            regular, regular, regular, regular,
         ],
         compiler_params=pltpu.CompilerParams(
             collective_id=0, has_side_effects=True, vmem_limit_bytes=60 * 1024 * 1024

time: 95.6 us -> 92.2 us (0.964)
  Pallas kernels: 94.7 us -> 91.3 us
    pallas_call x1, Pallas kernels: 91.6 us -> 88.2 us  [compute(): pl.pallas_call(comm_kernel, out_shape=OUTS, in_specs=[hbm] * 9, out_specs...]
where the time goes in v3:
time: 92.2 us; the launch traced here: 92.1 us
  Pallas kernels  91.3 us (99%)
    pallas_call x1, Pallas kernels, compute(): pl.pallas_call(comm_kernel, out_shape=OUTS, in_specs=[hbm] * 9, out_specs...  88.2 us
    pallas_call x1, Pallas kernels, place(): pl.pallas_call(place_kernel, out_shape=OUTS, in_specs=[hbm] * 6, out_spec...  3.08 us

profile of v3, /device:TPU:6, one launch (start us, length us, event | category | flops | bytes accessed | tf_op | source)
XLA Modules:
  0.0 92.1 jit_solution(11354164958417689048)
XLA Ops:
  0.6 88.2 %shard_map.136 = (bf16[192,256]{1,0:T(8,128)(2,1)}, f32[3696,128]{1,0:T(8,128)}, bf16[3696,128]{1,0:T(8,128)(2,1)}, bf16[3696,128]{1,0:T(8,128)(2,1)}, f32[2,1,924]{2,1,0:T(1,128)}, /*index=5*/f32[2,1,924]{2,1,0:T(1,128)}) custom-call(bf16[192,4096]{1,0:T(8,128)(2,1)} %x_hbm.1, bf16[192,924]{1,0:T(8,128)(2,1)} %gate_hbm.1, bf16[192,924]{1,0:T(8,128)(2,1)} %up_hbm.1, ...), custom_call_target="tpu_custom_call" | custom-call | flops 6000000000 | bytes 12000000 | tf_op jit(solution)/shard_map/pallas_call | solution.py:557
  88.9 3.1 %shard_map.137 = (bf16[192,256]{1,0:T(8,128)(2,1)}, f32[3696,128]{1,0:T(8,128)}, bf16[3696,128]{1,0:T(8,128)(2,1)}, bf16[3696,128]{1,0:T(8,128)(2,1)}, f32[2,1,924]{2,1,0:T(1,128)}, /*index=5*/f32[2,1,924]{2,1,0:T(1,128)}) custom-call(bf16[192,256]{1,0:T(8,128)(2,1)} %get-tuple-element.18.refs_0_, f32[3696,128]{1,0:T(8,128)} %get-tuple-element.19.refs_1_, ...), custom_call_target="tpu_custom_call" | custom-call | tf_op jit(solution)/shard_map/pallas_call | solution.py:643

commit v4 on v3

--- a/solution.py
+++ b/solution.py
@@ -74,7 +74,7 @@
     x_hbm, gate_hbm, up_hbm, gh_hbm, w_hbm, mc_hbm, sc_hbm, ms_hbm, ss_hbm,
     ig_out, step_out, mc_out, sc_out, ms_out, ss_out,
     gate_v, up_v, gh_v, w_v, w_f, mc_v, sc_v, ms_v, ss_v, ms_n, ss_n, m_f, s_f, step_v,
-    gbuf, fold, xbuf, xt, wt, dw_send, dw_recv, dw_own, c_send, c_recv, keep, rs_src, rs_recv, f_src, f_here, f_buf, out_v,
+    gbuf, fold, xbuf, xt, wt, dw_send, dw_recv, dw_own, c_send, c_recv, keep, before, rs_src, rs_recv, f_src, f_here, f_buf, out_v,
     load_sem, ring_s, ring_r, x1_s, x1_r, x2_s, x2_r, x3_s, x3_r, w_s, w_r,
     dw_s, dw_r, core_s, core_r, rs_s, rs_r, fz_s, fz_r, fin_s, fin_r, out_sem,
     z_near, z_far, y_near, plane_in,
@@ -376,10 +376,23 @@
     core_copies = {}
     rs_copies = {}
 
+    def dx_before():
+        block = gbuf[NZ - 1, :, :fold_at]
+        for which, j in ((0, 1 - c), (1, c)):
+            before[which] = jnp.dot(block, wt[j, :fold_at, :], preferred_element_type=F32)
+
+    def dx_after(which, j):
+        block = gbuf[NZ - 1, :, fold_at:]
+        product = jnp.dot(block, wt[j, fold_at:, :], preferred_element_type=F32)
+        return before[which] + product
+
     def dx_away(n):
         lo, hi = ROUNDS[n]
-        block = gbuf[lo:hi].reshape((hi - lo) * TOK, PACK)
-        there = jnp.dot(block, wt[1 - c], preferred_element_type=F32).astype(BF16)
+        if n == 4:
+            there = dx_after(0, 1 - c).astype(BF16)
+        else:
+            block = gbuf[lo:hi].reshape((hi - lo) * TOK, PACK)
+            there = jnp.dot(block, wt[1 - c], preferred_element_type=F32).astype(BF16)
         c_send[lo:hi] = there.reshape(hi - lo, TOK, 256)
         core_copies[n] = launch(remote(
             c_send.at[lo:hi], c_recv.at[lo:hi], core_s.at[n], core_r.at[n], sibling
@@ -387,6 +400,9 @@
 
     def dx_keep(n):
         lo, hi = ROUNDS[n]
+        if n == 4:
+            keep[lo:hi] = dx_after(1, c).reshape(1, TOK, 256)
+            return
         block = gbuf[lo:hi].reshape((hi - lo) * TOK, PACK)
         keep[lo:hi] = jnp.dot(block, wt[c], preferred_element_type=F32).reshape(hi - lo, TOK, 256)
 
@@ -510,7 +526,7 @@
     fourth(D)
     dw_out(D)
     step(E, 4)
-    dw_keep(D)
+    dx_before()
     third(E)
     unfold(3)
     dx_away(3)
@@ -522,6 +538,7 @@
     dw_out(E)
     dx_keep(4)
     dx_scatter(4)
+    dw_keep(D)
     dx_finish(2)
     dw_keep(E)
     dx_home(1)
@@ -585,6 +602,7 @@
             pltpu.VMEM((NZ, TOK, 256), BF16),
             pltpu.VMEM((NZ, TOK, 256), BF16),
             pltpu.VMEM((NZ, TOK, 256), F32),
+            pltpu.VMEM((2, TOK, 256), F32),
             pltpu.VMEM((NZ, TOK, 256), BF16),
             pltpu.VMEM((NY, NZ, QR, 256), BF16),
             pltpu.VMEM((NZ, QR, 256), BF16),
@@ -614,7 +632,7 @@
 
 
 PIECES = tuple(
-    (which, lo, min(lo + 1232, VIEW)) for lo in range(0, VIEW, 1232) for which in (1, 2, 3)
+    (which, lo, min(lo + 528, VIEW)) for lo in range(0, VIEW, 528) for which in (1, 2, 3)
 ) + ((0, 0, TOK), (4, 0, 2), (5, 0, 2))
 
 

time: 92.2 us -> 92.2 us (level)
  no operation moved by 1% of the time
where the time goes in v4:
time: 92.2 us; the launch traced here: 92.1 us
  Pallas kernels  91.3 us (99%)
    pallas_call x1, Pallas kernels, compute(): pl.pallas_call(comm_kernel, out_shape=OUTS, in_specs=[hbm] * 9, out_specs...  87.8 us
    pallas_call x1, Pallas kernels, place(): pl.pallas_call(place_kernel, out_shape=OUTS, in_specs=[hbm] * 6, out_spec...  3.56 us

profile of v4, /device:TPU:6, one launch (start us, length us, event | category | flops | bytes accessed | tf_op | source)
XLA Modules:
  0.0 92.1 jit_solution(7572182114925939056)
XLA Ops:
  0.6 87.8 %shard_map.136 = (bf16[192,256]{1,0:T(8,128)(2,1)}, f32[3696,128]{1,0:T(8,128)}, bf16[3696,128]{1,0:T(8,128)(2,1)}, bf16[3696,128]{1,0:T(8,128)(2,1)}, f32[2,1,924]{2,1,0:T(1,128)}, /*index=5*/f32[2,1,924]{2,1,0:T(1,128)}) custom-call(bf16[192,4096]{1,0:T(8,128)(2,1)} %x_hbm.1, bf16[192,924]{1,0:T(8,128)(2,1)} %gate_hbm.1, bf16[192,924]{1,0:T(8,128)(2,1)} %up_hbm.1, ...), custom_call_target="tpu_custom_call" | custom-call | flops 6000000000 | bytes 12000000 | tf_op jit(solution)/shard_map/pallas_call | solution.py:574
  88.4 3.6 %shard_map.137 = (bf16[192,256]{1,0:T(8,128)(2,1)}, f32[3696,128]{1,0:T(8,128)}, bf16[3696,128]{1,0:T(8,128)(2,1)}, bf16[3696,128]{1,0:T(8,128)(2,1)}, f32[2,1,924]{2,1,0:T(1,128)}, /*index=5*/f32[2,1,924]{2,1,0:T(1,128)}) custom-call(bf16[192,256]{1,0:T(8,128)(2,1)} %get-tuple-element.18.refs_0_, f32[3696,128]{1,0:T(8,128)} %get-tuple-element.19.refs_1_, ...), custom_call_target="tpu_custom_call" | custom-call | tf_op jit(solution)/shard_map/pallas_call | solution.py:661
